TPU v7x, 32 devices: a whole 2x2x4 slice. The times are simulated.
32 devices in a mesh: fsdp: 8 (over y, x, core), tensor: 4 (over z).
Axes of the slice: x: 2, y: 2, z: 4, core: 2. Of those that a mesh axis runs over, the one named last changes fastest.
Arguments:
- hidden_t: bfloat16 [28672, 512], P('fsdp', 'tensor'), may hold values from -6 to 6
- down_weight: bfloat16 [28672, 4096], P('fsdp', 'tensor'), may hold values from -0.03125 to 0.03125
- probe: bfloat16 [28672, 4096], P('fsdp', 'tensor'), may hold values from -5 to 5
- grad_moment: bfloat16 [28672, 4096], P('fsdp', 'tensor'), may hold values from -0.0059814453 to 0.0059814453
- curv_moment: bfloat16 [28672, 4096], P('fsdp', 'tensor'), may hold values from 0.0099487305 to 0.099609375
- target: bfloat16 [512, 4096], P('fsdp', 'tensor'), may hold values from -6 to 6
Outputs:
- new_grad_moment: bfloat16 [28672, 4096], P('fsdp', 'tensor')
- new_curv_moment: bfloat16 [28672, 4096], P('fsdp', 'tensor')
- update: bfloat16 [28672, 4096], P('fsdp', 'tensor')
All inputs are finite; a program needn't handle non-finite values.
Results may differ from a plain program's by a relative error of at most 0.0056.
Values may be sent and summed in bfloat16 or wider, within the bound.
A program may use at most 192 MiB of HBM per device.

v0:
```python
import jax
import jax.numpy as jnp
from jax import lax
from jax.sharding import PartitionSpec as P

BETA_ONE = 0.965
BETA_TWO = 0.99
RHO_SCALE = 0.02
EPS_FLOOR = 0.0005


def cotangents(summed, target_rows, col_width, token_count):
    adjoint = ((summed[:, :col_width] - target_rows.astype(jnp.float32)) / token_count).astype(
        jnp.bfloat16
    )
    tangent_adjoint = (summed[:, col_width:] / token_count).astype(jnp.bfloat16)
    return jnp.concatenate([adjoint, tangent_adjoint], axis=1)


def shards(hidden_t, down_weight, probe, grad_moment, curv_moment, target):
    gathered = lax.all_gather(hidden_t, "tensor", axis=1, tiled=True)
    col_width = down_weight.shape[1]
    token_count = gathered.shape[1]
    paired = jnp.concatenate([down_weight, probe], axis=1)
    partial_out = lax.dot_general(
        gathered, paired, (((0,), (0,)), ((), ())), preferred_element_type=jnp.float32
    )
    totals = lax.psum(partial_out, "fsdp")
    target_all = lax.all_gather(target, "fsdp", axis=0, tiled=True)
    stacked = cotangents(totals, target_all, col_width, token_count)
    products = jnp.dot(gathered, stacked, preferred_element_type=jnp.float32)
    gradient = products[:, :col_width]
    hess_probe = products[:, col_width:]
    estimate = probe.astype(jnp.float32) * hess_probe
    moment_next = BETA_ONE * grad_moment.astype(jnp.float32) + (1.0 - BETA_ONE) * gradient
    curv_next = BETA_TWO * curv_moment.astype(jnp.float32) + (1.0 - BETA_TWO) * estimate
    raw_ratio = moment_next / jnp.maximum(RHO_SCALE * curv_next, EPS_FLOOR)
    update = jnp.clip(raw_ratio, -1.0, 1.0)
    return (
        moment_next.astype(jnp.bfloat16),
        curv_next.astype(jnp.bfloat16),
        update.astype(jnp.bfloat16),
    )


def solution(mesh):
    in_specs = (
        P("fsdp", "tensor"),
        P("fsdp", "tensor"),
        P("fsdp", "tensor"),
        P("fsdp", "tensor"),
        P("fsdp", "tensor"),
        P("fsdp", "tensor"),
    )
    out_specs = (P("fsdp", "tensor"), P("fsdp", "tensor"), P("fsdp", "tensor"))
    return jax.shard_map(shards, mesh=mesh, in_specs=in_specs, out_specs=out_specs, check_vma=False)
```

profile of v0, /device:TPU:0, one launch (start us, length us, event | category | flops | bytes accessed | tf_op | source)
XLA Modules:
  0.0 273.3 jit_solution(6230435863053550682)
XLA Ops:
  7.2 0.0 all-gather.3.cloned.1.call-start
  7.2 0.7 all-gather.3.cloned.1.call-update
  7.9 0.0 all-gather.5.cloned.1.call-start
  7.9 0.7 all-gather.5.cloned.1.call-update
  8.6 0.0 all-reduce.2.cloned.1.call-start
  8.7 75.6 %all-gather.3.cloned.1.call-done = bf16[3584,512]{1,0:T(8,128)(2,1)} async-done(((bf16[3584,128]{1,0:T(8,128)(2,1)}), bf16[3584,512]{1,0:T(8,128)(2,1)}) %all-gather.3.cloned.1.call-update) | async-done | bytes 3670032 | tf_op jit(solution)/shard_map/all_gather | solution.py:21
  84.3 16.0 %fusion.8 = f32[512,2048]{0,1:T(8,128)} fusion(bf16[3584,512]{1,0:T(8,128)(2,1)} %all-gather.3.cloned.1.call-done, bf16[3584,1024]{1,0:T(8,128)(2,1)} %param.8, bf16[3584,1024]{1,0:T(8,128)(2,1)} %param.7), kind=kOutput, calls=%fused_computation.12 | convolution fusion | flops 7545552896 | bytes 22544384 | tf_op jit(solution)/shard_map/dot_general | solution.py:25
  100.3 0.0 all-reduce.2.cloned.1.call-update
  100.3 10.2 %copy.19 = bf16[3584,1024]{0,1:T(8,128)(2,1)} copy(bf16[3584,1024]{1,0:T(8,128)(2,1)} %param.8) | data formatting | bytes 14680064 | tf_op args[2]
  110.6 10.2 %copy.16 = bf16[3584,1024]{0,1:T(8,128)(2,1)} copy(bf16[3584,1024]{1,0:T(8,128)(2,1)} %param.9) | data formatting | bytes 14680064 | tf_op args[3]
  120.7 10.0 %copy.18 = bf16[3584,1024]{0,1:T(8,128)(2,1)} copy(bf16[3584,1024]{1,0:T(8,128)(2,1)} %param.10) | data formatting | bytes 14680064 | tf_op args[4]
  130.8 0.0 all-gather.5.cloned.1.call-done
  130.8 1.5 copy.17
  132.3 59.9 %all-reduce.2.cloned.1.call-done = f32[512,2048]{0,1:T(8,128)} async-done(((f32[512,2048]{0,1:T(8,128)}), f32[512,2048]{0,1:T(8,128)}) %all-reduce.2.cloned.1.call-update) | async-done | bytes 4194320 | tf_op jit(solution)/shard_map/psum | solution.py:28
  192.2 0.0 slice-start
  192.2 3.0 %fusion.14 = (bf16[512,1024]{0,1:T(8,128)(2,1)S(1)}, bf16[512,1024]{0,1:T(8,128)(2,1)S(1)}) fusion(f32[512,2048]{0,1:T(8,128)} %all-reduce.2.cloned.1.call-done, bf16[512,1024]{0,1:T(8,128)(2,1)S(1)} %copy.17), kind=kLoop, calls=%fused_computation.18 | loop fusion | flops 3145728 | bytes 7340032 | tf_op jit(solution)/shard_map/convert_element_type | solution.py:13
  195.2 0.0 slice-start.1
  195.3 16.8 %convolution_bitcast_fusion = f32[3584,2048]{0,1:T(8,128)} fusion(bf16[3584,512]{1,0:T(8,128)(2,1)} %all-gather.3.cloned.1.call-done, bf16[512,1024]{0,1:T(8,128)(2,1)S(1)} %get-tuple-element.13, bf16[512,1024]{0,1:T(8,128)(2,1)S(1)} %get-tuple-element.12), kind=kOutput, calls=%fused_computation | convolution fusion | flops 7520387072 | bytes 35127296 | tf_op jit(solution)/shard_map/dot_general | solution.py:31
  212.1 0.0 slice-done
  212.1 0.0 slice-done.1
  212.1 23.6 %clamp_convert_fusion = (bf16[3584,1024]{0,1:T(8,128)(2,1)}, bf16[3584,1024]{0,1:T(8,128)(2,1)}, bf16[3584,1024]{0,1:T(8,128)(2,1)}) fusion(f32[3584,2048]{0,1:T(8,128)} %convolution_bitcast_fusion, bf16[3584,1024]{0,1:T(8,128)(2,1)} %copy.16, bf16[3584,1024]{0,1:T(8,128)(2,1)S(1)} %bitcast.7, bf16[3584,1024]{0,1:T(8,128)(2,1)} %copy.18), kind=kLoop, calls=%fused_computation.10 | loop fusion | flops 62390272 | bytes 73400320 | tf_op jit(solution)/shard_map/convert_element_type | solution.py:42
  235.6 10.4 %copy.20 = bf16[3584,1024]{1,0:T(8,128)(2,1)} copy(bf16[3584,1024]{0,1:T(8,128)(2,1)} %get-tuple-element.11) | data formatting | bytes 14680064
  246.0 10.4 %copy.21 = bf16[3584,1024]{1,0:T(8,128)(2,1)} copy(bf16[3584,1024]{0,1:T(8,128)(2,1)} %get-tuple-element.10) | data formatting | bytes 14680064
  256.4 10.4 %copy.22 = bf16[3584,1024]{1,0:T(8,128)(2,1)} copy(bf16[3584,1024]{0,1:T(8,128)(2,1)} %get-tuple-element.9) | data formatting | bytes 14680064
  (1 shorter events, 0.0 us)
Async XLA Ops:
  7.2 77.1 %all-gather.3.cloned.1.call-start = ((), (), s32[]{:S(2)}) async-start(), calls=%async_computation | async-start | bytes 4587520 | tf_op jit(solution)/shard_map/all_gather | solution.py:21
  7.9 122.9 %all-gather.5.cloned.1.call-start = ((), (), s32[]{:S(2)}) async-start(), calls=%async_computation.2 | async-start | bytes 1179648 | tf_op jit(solution)/shard_map/all_gather | solution.py:29
  8.6 183.6 %all-reduce.2.cloned.1.call-start = ((), (), s32[]{:S(2)}) async-start(), calls=%async_computation.1 | async-start | bytes 8388608 | tf_op jit(solution)/shard_map/psum | solution.py:28
  192.2 19.9 %slice-start = ((s8[7340032]{0:T(1024)(128)(4,1)}), s8[4194304]{0:T(1024)(128)(4,1)S(1)}, s32[]{:S(2)}) async-start(s8[7340032]{0:T(1024)(128)(4,1)} %bitcast.6), calls=%async_computation.3 | async-start | bytes 8388608
  195.2 16.8 %slice-start.1 = ((s8[7340032]{0:T(1024)(128)(4,1)}), s8[3145728]{0:T(1024)(128)(4,1)S(1)}, s32[]{:S(2)}) async-start(s8[7340032]{0:T(1024)(128)(4,1)} %bitcast.6), calls=%async_computation.4 | async-start | bytes 6291456
Sparse Core Ops, SparseCore 0:
  9.6 74.6 all-gather.2
  86.2 21.6 all-gather.4
  111.2 80.9 all-reduce.1
where the time goes:
time: 275 us; the launch traced here: 273 us
  waiting for transfers between devices  137 us (50%)
  local copies, waits for them, and re-layouts  63.2 us (23%)
  matrix products  32.8 us (12%)
  other arithmetic  26.6 us (10%)
  between operations  13.8 us (5%)
    all_gather x1, waiting for transfers between devices, shards(): gathered = lax.all_gather(hidden_t, 'tensor', axis=1, tiled=True)  75.6 us
    unnamed x10, local copies, waits for them, and re-layouts  61.7 us
    psum x1, waiting for transfers between devices, shards(): totals = lax.psum(partial_out, 'fsdp')  59.9 us
    convert_element_type x1, other arithmetic, shards(): update.astype(jnp.bfloat16)  23.6 us
    dot_general x1, matrix products, shards(): products = jnp.dot(gathered, stacked, preferred_element_type=jnp.float32)  16.8 us
    dot_general x1, matrix products, shards(): lax.dot_general(gathered, paired, (((0,), (0,)), ((), ())), preferred_ele...  16 us
  transfers between devices with their start and end apart: 3, of which 2 were waited for; matrix products, arithmetic and copies ran while one was open for 18% of the time, Pallas kernels for 0%

commit v1 on v0

--- a/solution.py
+++ b/solution.py
@@ -9,6 +9,19 @@
 EPS_FLOOR = 0.0005
 
 
+def collect(shard, axis, dim):
+    ways = lax.axis_size(axis)
+    up = [(d, (d + 1) % ways) for d in range(ways)]
+    down = [(d, (d - 1) % ways) for d in range(ways)]
+    earlier, later = ([shard], [shard])
+    for _ in range(ways // 2):
+        earlier.append(lax.ppermute(earlier[-1], axis, up))
+    for _ in range((ways - 1) // 2):
+        later.append(lax.ppermute(later[-1], axis, down))
+    line = jnp.concatenate([*earlier[::-1], *later[1:]], axis=dim)
+    return jnp.roll(line, (lax.axis_index(axis) - ways // 2) * shard.shape[dim], axis=dim)
+
+
 def cotangents(summed, target_rows, col_width, token_count):
     adjoint = ((summed[:, :col_width] - target_rows.astype(jnp.float32)) / token_count).astype(
         jnp.bfloat16
@@ -18,7 +31,7 @@
 
 
 def shards(hidden_t, down_weight, probe, grad_moment, curv_moment, target):
-    gathered = lax.all_gather(hidden_t, "tensor", axis=1, tiled=True)
+    gathered = collect(hidden_t, "tensor", 1)
     col_width = down_weight.shape[1]
     token_count = gathered.shape[1]
     paired = jnp.concatenate([down_weight, probe], axis=1)

time: 275 us -> 227 us (0.83)
  local copies, waits for them, and re-layouts: 63.2 us -> 16.1 us
  starting transfers between devices: 0.11 us -> 6.98 us
  matrix products: 32.8 us -> 29 us
    all_gather x1 -> x0, waiting for transfers between devices: 75.6 us -> none  [shards(): gathered = lax.all_gather(hidden_t, 'tensor', axis=1, tiled=True)]
    ppermute x0 -> x3, waiting for transfers between devices: none -> 53.8 us  [the longest x2 44.2 us: collect(): earlier.append(lax.ppermute(earlier[-1], axis, up))]
    unnamed x10 -> x21, local copies, waits for them, and re-layouts: 61.7 us -> 14 us
    psum x1, waiting for transfers between devices: 59.9 us -> 81 us  [shards(): totals = lax.psum(partial_out, 'fsdp')]
    ppermute x0 -> x3, starting transfers between devices: none -> 6.9 us  [the longest x1 3.82 us: collect(): later.append(lax.ppermute(later[-1], axis, down))]
  transfers between devices with their start and end apart: 3 -> 5, of which waited for: 2 -> 4; matrix products, arithmetic and copies ran while one was open for 18% -> 13% of each run, Pallas kernels for 0% -> 0%
where the time goes in v1:
time: 227 us; the launch traced here: 226 us
  waiting for transfers between devices  135 us (59%)
  matrix products  29 us (13%)
  other arithmetic  25.2 us (11%)
  local copies, waits for them, and re-layouts  16.1 us (7%)
  between operations  14.1 us (6%)
  starting transfers between devices  6.98 us (3%)
    psum x1, waiting for transfers between devices, shards(): totals = lax.psum(partial_out, 'fsdp')  81 us
    ppermute x2, waiting for transfers between devices, collect(): earlier.append(lax.ppermute(earlier[-1], axis, up))  44.2 us
    convert_element_type x1, other arithmetic, shards(): update.astype(jnp.bfloat16)  20.9 us
    dot_general x1, matrix products, shards(): products = jnp.dot(gathered, stacked, preferred_element_type=jnp.float32)  15.5 us
    unnamed x21, local copies, waits for them, and re-layouts  14 us
    dot_general x1, matrix products, shards(): lax.dot_general(gathered, paired, (((0,), (0,)), ((), ())), preferred_ele...  13.5 us
    ppermute x1, waiting for transfers between devices, collect(): later.append(lax.ppermute(later[-1], axis, down))  9.63 us
  transfers between devices with their start and end apart: 5, of which 4 were waited for; matrix products, arithmetic and copies ran while one was open for 13% of the time, Pallas kernels for 0%

profile of v1, /device:TPU:0, one launch (start us, length us, event | category | flops | bytes accessed | tf_op | source)
XLA Modules:
  0.0 226.2 jit_solution(12162489615949591926)
XLA Ops:
  7.2 0.0 all-gather.2.cloned.1.call-start
  7.2 3.1 %collective-permute-start = (bf16[3584,128]{1,0:T(8,128)(2,1)}, bf16[3584,128]{1,0:T(8,128)(2,1)}, u32[]{:S(2)}, u32[]{:S(2)}) collective-permute-start(bf16[3584,128]{1,0:T(8,128)(2,1)} %param.6), channel_id=1, source_target_pairs={{0,1},{1,2},{2,3},{3,0},{4,5},{5,6},{6,7},{7,4},{8,9},{9,10},{10,1... | collective-permute-start | bytes 2752520 | tf_op jit(solution)/shard_map/ppermute | solution.py:18
  10.3 22.7 %collective-permute-done = bf16[3584,128]{1,0:T(8,128)(2,1)} collective-permute-done((bf16[3584,128]{1,0:T(8,128)(2,1)}, bf16[3584,128]{1,0:T(8,128)(2,1)}, u32[]{:S(2)}, u32[]{:S(2)}) %collective-permute-start) | collective-permute-done | bytes 917536 | tf_op jit(solution)/shard_map/ppermute | solution.py:18
  33.0 0.0 collective-permute-start.1
  33.0 3.8 %collective-permute-start.2 = (bf16[3584,128]{1,0:T(8,128)(2,1)}, bf16[3584,128]{1,0:T(8,128)(2,1)}, u32[]{:S(2)}, u32[]{:S(2)}) collective-permute-start(bf16[3584,128]{1,0:T(8,128)(2,1)} %param.6), channel_id=1, source_target_pairs={{0,3},{1,0},{2,1},{3,2},{4,7},{5,4},{6,5},{7,6},{8,11},{9,8},{10,9... | collective-permute-start | bytes 2752520 | tf_op jit(solution)/shard_map/ppermute | solution.py:20
  36.8 0.0 all-gather.2.cloned.1.call-update
  36.8 0.0 all-reduce.2.cloned.1.call-start
  36.9 0.0 slice-start
  36.9 0.0 copy-start
  36.9 21.5 %collective-permute-done.1 = bf16[3584,128]{1,0:T(8,128)(2,1)} collective-permute-done((bf16[3584,128]{1,0:T(8,128)(2,1)}, bf16[3584,128]{1,0:T(8,128)(2,1)}, u32[]{:S(2)}, u32[]{:S(2)}) %collective-permute-start.1) | collective-permute-done | bytes 917536 | tf_op jit(solution)/shard_map/ppermute | solution.py:18
  58.4 2.2 constant_dynamic-update-slice_fusion.7
  60.5 2.2 constant_dynamic-update-slice_fusion.6
  62.7 2.2 constant_dynamic-update-slice_fusion.5
  64.9 9.6 %collective-permute-done.2 = bf16[3584,128]{1,0:T(8,128)(2,1)} collective-permute-done((bf16[3584,128]{1,0:T(8,128)(2,1)}, bf16[3584,128]{1,0:T(8,128)(2,1)}, u32[]{:S(2)}, u32[]{:S(2)}) %collective-permute-start.2) | collective-permute-done | bytes 917536 | tf_op jit(solution)/shard_map/ppermute | solution.py:20
  74.5 2.2 constant_dynamic-update-slice_fusion.4
  76.7 2.2 constant_dynamic-update-slice_fusion.3
  78.8 2.2 constant_dynamic-update-slice_fusion.2
  81.0 0.0 copy-done
  81.0 1.0 constant_dynamic-update-slice_fusion.1
  82.0 2.2 constant_dynamic-update-slice_fusion
  84.1 0.0 slice-done
  84.1 0.0 slice-done.1
  84.1 13.5 %fusion.3 = f32[512,2048]{1,0:T(8,128)} fusion(bf16[3584,1024]{1,0:T(8,128)(2,1)S(1)} %bitcast.1, bf16[3584,1024]{1,0:T(8,128)(2,1)} %param.7, bf16[3584,1024]{1,0:T(8,128)(2,1)} %constant_dynamic-update-slice_fusion, s32[]{:T(128)S(6)} %select_n.14), kind=kOutput, calls=%fused_computation.5 | convolution fusion | flops 7545552896 | bytes 22544388 | tf_op jit(solution)/shard_map/dot_general | solution.py:38
  97.7 0.0 all-reduce.2.cloned.1.call-update
  97.7 0.0 all-gather.2.cloned.1.call-done
  97.7 81.0 %all-reduce.2.cloned.1.call-done = f32[512,2048]{1,0:T(8,128)} async-done(((f32[512,2048]{1,0:T(8,128)}), f32[512,2048]{1,0:T(8,128)}) %all-reduce.2.cloned.1.call-update) | async-done | bytes 4194320 | tf_op jit(solution)/shard_map/psum | solution.py:41
  178.7 4.3 %fusion.14 = (bf16[512,1024]{1,0:T(8,128)(2,1)S(1)}, bf16[512,1024]{1,0:T(8,128)(2,1)}) fusion(f32[512,2048]{1,0:T(8,128)} %all-reduce.2.cloned.1.call-done, bf16[512,1024]{1,0:T(8,128)(2,1)} %all-gather.2.cloned.1.call-done), kind=kLoop, calls=%fused_computation.19 | loop fusion | flops 3145728 | bytes 7340032 | tf_op jit(solution)/shard_map/convert_element_type | solution.py:26
  183.0 15.5 %fusion.8 = f32[3584,2048]{1,0:T(8,128)} fusion(bf16[3584,1024]{1,0:T(8,128)(2,1)} %constant_dynamic-update-slice_fusion, s32[]{:T(128)S(6)} %select_n.14, bf16[512,1024]{1,0:T(8,128)(2,1)} %get-tuple-element.7, bf16[512,1024]{1,0:T(8,128)(2,1)S(1)} %get-tuple-element.6), kind=kOutput, calls=%fused_computation.11 | convolution fusion | flops 7520387072 | bytes 35127300 | tf_op jit(solution)/shard_map/dot_general | solution.py:44
  198.4 0.0 slice-done.2
  198.4 0.0 slice-done.4
  198.4 0.0 slice-done.3
  198.5 20.9 %clamp_convert_fusion = (bf16[3584,1024]{1,0:T(8,128)(2,1)}, bf16[3584,1024]{1,0:T(8,128)(2,1)}, bf16[3584,1024]{1,0:T(8,128)(2,1)}) fusion(f32[3584,2048]{1,0:T(8,128)} %fusion.8, bf16[3584,1024]{1,0:T(8,128)(2,1)S(1)} %bitcast.5, bf16[3584,1024]{1,0:T(8,128)(2,1)S(1)} %bitcast.3, bf16[3584,1024]{1,0:T(8,128)(2,1)} %param.10), kind=kLoop, calls=%fused_computation.9 | loop fusion | flops 62390272 | bytes 73400320 | tf_op jit(solution)/shard_map/convert_element_type | solution.py:55
  (9 shorter events, 0.0 us)
Async XLA Ops:
  7.2 90.6 %all-gather.2.cloned.1.call-start = ((), (), s32[]{:S(2)}) async-start(), calls=%async_computation.1 | async-start | bytes 1179648 | tf_op jit(solution)/shard_map/all_gather | solution.py:42
  7.2 25.8 %collective-permute-start = (bf16[3584,128]{1,0:T(8,128)(2,1)}, bf16[3584,128]{1,0:T(8,128)(2,1)}, u32[]{:S(2)}, u32[]{:S(2)}) collective-permute-start(bf16[3584,128]{1,0:T(8,128)(2,1)} %param.6), channel_id=1, source_target_pairs={{0,1},{1,2},{2,3},{3,0},{4,5},{5,6},{6,7},{7,4},{8,9},{9,10},{10,1... | collective-permute-start | bytes 2752520 | tf_op jit(solution)/shard_map/ppermute | solution.py:18
  33.0 25.4 %collective-permute-start.1 = (bf16[3584,128]{1,0:T(8,128)(2,1)}, bf16[3584,128]{1,0:T(8,128)(2,1)}, u32[]{:S(2)}, u32[]{:S(2)}) collective-permute-start(bf16[3584,128]{1,0:T(8,128)(2,1)} %collective-permute-done), channel_id=1, source_target_pairs={{0,1},{1,2},{2,3},{3,0},{4,5},{5,6},{6,7},{7,4},{8,9},{9,10},{10,1... | collective-permute-start | bytes 2752520 | tf_op jit(solution)/shard_map/ppermute | solution.py:18
  33.0 41.5 %collective-permute-start.2 = (bf16[3584,128]{1,0:T(8,128)(2,1)}, bf16[3584,128]{1,0:T(8,128)(2,1)}, u32[]{:S(2)}, u32[]{:S(2)}) collective-permute-start(bf16[3584,128]{1,0:T(8,128)(2,1)} %param.6), channel_id=1, source_target_pairs={{0,3},{1,0},{2,1},{3,2},{4,7},{5,4},{6,5},{7,6},{8,11},{9,8},{10,9... | collective-permute-start | bytes 2752520 | tf_op jit(solution)/shard_map/ppermute | solution.py:20
  36.8 141.9 %all-reduce.2.cloned.1.call-start = ((), (), s32[]{:S(2)}) async-start(), calls=%async_computation | async-start | bytes 8388608 | tf_op jit(solution)/shard_map/psum | solution.py:41
  36.9 47.2 %slice-start = ((s8[7340032]{0:T(1024)(128)(4,1)}), s8[3145728]{0:T(1024)(128)(4,1)S(1)}, s32[]{:S(2)}) async-start(s8[7340032]{0:T(1024)(128)(4,1)} %bitcast), calls=%async_computation.2 | async-start | bytes 6291456
  36.9 44.1 %copy-start = (bf16[3584,128]{1,0:T(8,128)(2,1)S(1)}, bf16[3584,128]{1,0:T(8,128)(2,1)}, u32[]{:S(2)}) copy-start(bf16[3584,128]{1,0:T(8,128)(2,1)} %param.6) | copy-start | bytes 2752516
  64.9 19.3 %slice-start.1 = ((s8[7340032]{0:T(1024)(128)(4,1)}), s8[4194304]{0:T(1024)(128)(4,1)S(1)}, s32[]{:S(2)}) async-start(s8[7340032]{0:T(1024)(128)(4,1)} %bitcast), calls=%async_computation.3 | async-start | bytes 8388608
  178.7 19.8 %slice-start.2 = ((s8[7340032]{0:T(1024)(128)(4,1)}), s8[4194304]{0:T(1024)(128)(4,1)S(1)}, s32[]{:S(2)}) async-start(s8[7340032]{0:T(1024)(128)(4,1)} %bitcast.2), calls=%async_computation.4 | async-start | bytes 8388608
  178.7 19.8 %slice-start.4 = ((s8[7340032]{0:T(1024)(128)(4,1)}), s8[4194304]{0:T(1024)(128)(4,1)S(1)}, s32[]{:S(2)}) async-start(s8[7340032]{0:T(1024)(128)(4,1)} %bitcast.4), calls=%async_computation.6 | async-start | bytes 8388608
  183.0 15.5 %slice-start.3 = ((s8[7340032]{0:T(1024)(128)(4,1)}), s8[3145728]{0:T(1024)(128)(4,1)S(1)}, s32[]{:S(2)}) async-start(s8[7340032]{0:T(1024)(128)(4,1)} %bitcast.2), calls=%async_computation.5 | async-start | bytes 6291456
  183.0 15.5 %slice-start.5 = ((s8[7340032]{0:T(1024)(128)(4,1)}), s8[3145728]{0:T(1024)(128)(4,1)S(1)}, s32[]{:S(2)}) async-start(s8[7340032]{0:T(1024)(128)(4,1)} %bitcast.4), calls=%async_computation.7 | async-start | bytes 6291456
Sparse Core Ops, SparseCore 0:
  36.9 21.6 all-gather.1
  97.8 80.8 all-reduce.1
